TPU v7x, 32 devices: a whole 2x2x4 slice. The times are simulated.
32 devices in a mesh: energy: 4 (over z), slab: 8 (over y, x, core).
Axes of the slice: x: 2, y: 2, z: 4, core: 2. Of those that a mesh axis runs over, the one named last changes fastest.
Arguments:
- wavefunction: bfloat16 [4, 128, 64, 256], P('energy', 'slab'), may hold values from -6 to 6
- injected_modes: int32 [4, 64], P('energy'), may hold values from 0 to 255, all different within a row
- factor_blocks: float32 [4, 128, 256, 256], P('energy', 'slab'), may hold values from -1.1 to 1.1
- pivot_inverse: float32 [4, 128, 256, 256], P('energy', 'slab'), may hold values from -1 to 2.5
- mode_velocity: float32 [4, 256], P('energy'), may hold values from 0.1 to 1
- energy_weight: float32 [4], P('energy'), may hold values from 0.5 to 8
- mode_basis: bfloat16 [256, 1024], replicated, may hold values from -0.375 to 0.375
Outputs:
- sensitivity: float32 [1024, 128], P('energy', 'slab')
Inputs may be any that keep to these rules, and one draw needn't show every extreme that they name: `injected_modes`: each energy's row names 64 different modes, and every mode is named by some energy.
All inputs are finite; a program needn't handle non-finite values.
Results may differ from a plain program's by a relative error of at most 0.0003.
Values sent between devices are 32-bit elements; how exact they have to be, the bound alone decides.
A program may use at most 128 MiB of HBM per device.

v0:
```python
import functools
import jax
import jax.numpy as jnp
from jax import lax
from jax.experimental import pallas as pl
from jax.experimental.pallas import tpu as pltpu
from jax.sharding import PartitionSpec as P

F32 = jnp.float32
BF16 = jnp.bfloat16
MESH = pl.DeviceIdType.MESH


def split(x):
    hi = x.astype(BF16)
    return hi, (x - hi.astype(F32)).astype(BF16)


def dot(a, b, transposed=False):
    return lax.dot_general(
        a, b, (((1,), (1 if transposed else 0,)), ((), ())), preferred_element_type=F32
    )


def mm(a, bh, bl, transposed=False):
    ah, al = split(a)
    rows = a.shape[0]
    both = dot(jnp.concatenate([ah, al], axis=0), bh, transposed)
    return both[:rows] + both[rows:] + dot(ah, bl, transposed)


def kernel(
    n, groups,
    wave, inj, fac_hbm, piv_hbm, vel, ew, basis,
    out,
    fac, piv, ahl, fac_sem, piv_sem, tah, tal, whole_off, incb,
    fh, fl, qh, ql, uh, ul, th, tl, state, wt, adj, wg, off, scaled_ref,
    inc, cur, ctot, ps, pr, osend, orecv, tsend, trecv, isend, irecv, xsend, xrecv,
    ysend, yrecv, jsend, jrecv, esend, erecv,
    pair_s, pair_r, os, our, ts, tr, is_, ir, xs, xr, ys, yr, js, jr, es, er,
):
    me = lax.axis_index("slab")
    mine = lax.axis_index("energy")
    slabs, cols, modes = wave.shape
    grid = basis.shape[1]
    part = grid // groups
    chips = n // 2
    chip = me // 2
    core = lax.rem(me, 2)
    other = me + 1 - 2 * core
    total = modes + cols
    half = slabs // 2
    all_slabs = n * slabs
    small = 2.0 / (all_slabs * cols * modes * groups * 4096.0)

    def factor_in(s):
        return pltpu.make_async_copy(fac_hbm.at[s], fac.at[s], fac_sem.at[s])

    for s in range(half):
        factor_in(s).start()
        factor_in(half + s).start()
    pivots_in = pltpu.make_async_copy(piv_hbm, piv, piv_sem)
    pivots_in.start()

    barrier = pltpu.get_barrier_semaphore()

    for k in range(1, n):
        pl.semaphore_signal(
            barrier, inc=1, device_id=(mine, lax.rem(me + k, n)), device_id_type=MESH
        )
    for k in range(1, groups):
        peer = lax.rem(mine + k, groups)
        pl.semaphore_signal(barrier, inc=1, device_id=(peer, me), device_id_type=MESH)

    rows_at = lax.broadcasted_iota(jnp.int32, (cols, cols), 0)
    cols_at = lax.broadcasted_iota(jnp.int32, (cols, cols), 1)
    picked = jnp.sum(
        jnp.where(rows_at == cols_at, jnp.broadcast_to(inj[...].astype(F32), (cols, cols)), 0.0),
        axis=1, keepdims=True,
    )
    mode_at = lax.broadcasted_iota(jnp.int32, (cols, modes), 1).astype(F32)
    velocity = jnp.broadcast_to(vel[...], (cols, modes))
    at_injected = jnp.sum(jnp.where(mode_at == picked, velocity, 0.0), axis=1, keepdims=True)
    scaled_ref[...] = ew[...] * (1.0 / at_injected) * velocity

    eye = (
        lax.broadcasted_iota(jnp.int32, (modes, modes), 0)
        == lax.broadcasted_iota(jnp.int32, (modes, modes), 1)
    ).astype(F32)

    for k in range(2):
        off[k, 0:modes] = eye
        off[k, modes:] = jnp.zeros((cols, modes), F32)
    cur[...] = jnp.zeros_like(cur)

    def chain(t, carry):
        blocks = []
        for k in range(2):
            s = k * half + t
            w = wave[s].astype(F32)
            sw = scaled_ref[...] * w
            sq = sw * w
            part_sum = sq[0:8]
            for i in range(1, cols // 8):
                part_sum = part_sum + sq[8 * i : 8 * i + 8]
            tile = part_sum[:, 0:128]
            for i in range(1, modes // 128):
                tile = tile + part_sum[:, 128 * i : 128 * i + 128]
            cur[...] += tile
            own = off[k, modes:] + sw * small
            state[s] = own
            bh, bl = split(jnp.concatenate([off[k, 0:modes], own], axis=0))
            qh[s] = bh[0:modes]
            ql[s] = bl[0:modes]
            factor_in(s).wait()
            h, l = split(fac[s])
            fh[s] = h
            fl[s] = l
            blocks.append((bh, bl, h, l))
        results = []
        for bh, bl, h, l in blocks:
            both = dot(jnp.concatenate([bh, bl], axis=0), h)
            results.append(both[:total] + both[total:] + dot(bh, l))
        for k in range(2):
            off[k] = results[k]
        return carry

    lax.fori_loop(0, half, chain, 0, unroll=2)
    h, l = split(off[0, 0:modes])
    tah[...] = h
    tal[...] = l
    h, l = split(off[1, 0:modes])
    joined = mm(off[0], h, l)
    h, l = split(joined[0:modes])
    th[...] = h
    tl[...] = l
    whole_off[...] = joined[modes:] + off[1, modes:]
    ps[0:modes] = joined[0:modes]
    ps[modes:total] = whole_off[...]

    pl.semaphore_wait(barrier, n + groups - 2)

    def copy_to(source, target, send, receive, device):
        return pltpu.make_async_remote_copy(
            src_ref=source, dst_ref=target, send_sem=send, recv_sem=receive,
            device_id=(mine, device), device_id_type=MESH,
        )

    pair = copy_to(ps, pr, pair_s, pair_r, other)
    entry = copy_to(isend, irecv, is_, ir, other)
    leaving = copy_to(xsend, xrecv, xs, xr, other)
    joining = copy_to(jsend, jrecv, js, jr, other)

    def offset_to(j):
        return copy_to(osend, orecv.at[chip], os.at[j], our.at[chip], 2 * j + 1)

    def transfer_to(j, k):
        return copy_to(tsend, trecv.at[chip], ts.at[j], tr.at[chip], 2 * j + k)

    def exit_to(j):
        return copy_to(ysend, yrecv.at[chip], ys.at[j], yr.at[chip], 2 * j)

    def wait_transfer(j):
        copy_to(tsend, trecv.at[j], ts.at[j], tr.at[j], other).wait_recv()

    def wait_offset(j):
        copy_to(osend, orecv.at[j], os.at[j], our.at[j], other).wait_recv()

    def wait_exit(j):
        copy_to(ysend, yrecv.at[j], ys.at[j], yr.at[j], other).wait_recv()

    def put(ref, value, tile):
        ref[0:cols] = value
        ref[cols : cols + 8, 0:128] = tile
        ref[cols : cols + 8, 128:] = jnp.zeros((8, modes - 128), F32)

    inner = jnp.logical_and(chip > 0, chip < chips - 1)

    ps[total:, 0:128] = cur[...]
    ps[total:, 128:] = jnp.zeros((8, modes - 128), F32)
    pair.start()
    pair.wait_recv()
    cur[...] += pr[total:, 0:128]
    ctot[...] = cur[...]

    @pl.when(core == 1)
    def _():
        whole = mm(pr[0:total], th[...], tl[...])
        tsend[...] = whole[0:modes]
        put(osend, whole[modes:] + whole_off[...], cur[...])
        for j in range(chips):
            @pl.when(j > chip)
            def _():
                offset_to(j).start()

        @pl.when(inner)
        def _():
            for j in range(chips):
                @pl.when(j > chip)
                def _():
                    transfer_to(j, 1).start()

    for k in range(2):
        off[k, 0:modes] = eye

    def suffix(i, carry):
        results = []
        for k in range(2):
            s = k * half + half - 1 - i
            results.append(mm(off[k, 0:modes], fh[s], fl[s], True))
        for k in range(2):
            s = k * half + half - 1 - i
            off[k, 0:modes] = results[k]
            h, l = split(results[k])
            uh[s] = h
            ul[s] = l
        return carry

    lax.fori_loop(0, half, suffix, 0, unroll=2)

    @pl.when(jnp.logical_and(core == 1, inner))
    def _():
        for j in range(chips):
            @pl.when(j < chip)
            def _():
                transfer_to(j, 0).start()

    inc[...] = jnp.zeros_like(inc)

    @pl.when(core == 1)
    def _():
        for j in range(chips - 1):
            @pl.when(chip > j)
            def _():
                if j > 0:
                    wait_transfer(j)
                wait_offset(j)
                if j == 0:
                    inc[...] = orecv[j, 0:cols]
                else:
                    h, l = split(trecv[j])
                    inc[...] = mm(inc[...], h, l) + orecv[j, 0:cols]
                ctot[...] += orecv[j, cols : cols + 8, 0:128]

        put(isend, inc[...], ctot[...])
        entry.start()
        h, l = split(pr[0:modes])
        inc[...] = mm(inc[...], h, l) + pr[modes:total]

    @pl.when(core == 0)
    def _():
        entry.wait_recv()
        inc[...] = irecv[0:cols]
        ctot[...] = irecv[cols : cols + 8, 0:128]

    pivots_in.wait()

    incb[...] = mm(inc[...], tah[...], tal[...]) + off[0, modes:]

    def weigh(t, leaves):
        left = []
        for k, entering in enumerate((inc, incb)):
            s = k * half + t
            now = state[s] + mm(entering[...], qh[s], ql[s])
            h, l = split(piv[s])
            weighted = mm(now, h, l)
            wt[s] = weighted
            left.append(leaves[k] + mm(weighted, qh[s], ql[s], True))
        return tuple(left)

    nothing = jnp.zeros((cols, modes), F32)
    leaves = lax.fori_loop(0, half, weigh, (nothing, nothing), unroll=2)
    exit_state = leaves[0] + mm(leaves[1], tah[...], tal[...], True)

    @pl.when(core == 1)
    def _():
        xsend[...] = exit_state
        leaving.start()

    @pl.when(core == 0)
    def _():
        leaving.wait_recv()

        @pl.when(chip > 0)
        def _():
            put(ysend, exit_state + mm(xrecv[...], th[...], tl[...], True), cur[...])
            for j in range(chips):
                @pl.when(j < chip)
                def _():
                    exit_to(j).start()

    def back(i, held):
        left = []
        for k in range(2):
            s = k * half + half - 1 - i
            x = wt[s] + mm(held[k], fh[s], fl[s], True)
            adj[s] = x
            left.append(x)
        return tuple(left)

    lax.fori_loop(0, half, back, (nothing, nothing), unroll=2)

    def waves(b, carry):
        wg[b] = dot(wave[pl.ds(4 * b, 4)].reshape(4 * cols, modes), basis[...])
        return carry

    lax.fori_loop(0, slabs // 4, waves, 0)

    @pl.when(core == 0)
    def _():
        inc[...] = jnp.zeros_like(inc)
        for j in range(chips - 1, 0, -1):
            @pl.when(chip < j)
            def _():
                if j < chips - 1:
                    wait_transfer(j)
                wait_exit(j)
                if j == chips - 1:
                    inc[...] = yrecv[j, 0:cols]
                else:
                    h, l = split(trecv[j])
                    inc[...] = mm(inc[...], h, l, True) + yrecv[j, 0:cols]
                ctot[...] += yrecv[j, cols : cols + 8, 0:128]

        put(jsend, inc[...], ctot[...])
        joining.start()
        h, l = split(pr[0:modes])
        inc[...] = mm(inc[...], h, l, True) + xrecv[...]

    @pl.when(core == 1)
    def _():
        joining.wait_recv()
        inc[...] = jrecv[0:cols]
        ctot[...] = jrecv[cols : cols + 8, 0:128]

    incb[...] = adj[half] + mm(inc[...], uh[half], ul[half])

    for b in range(slabs // 4):
        for i in range(4):
            s = 4 * b + i
            entering = incb if s < half else inc
            h, l = split(adj[s] + mm(entering[...], uh[s], ul[s]))
            ahl[b, cols * i : cols * (i + 1)] = h
            ahl[b, cols * (4 + i) : cols * (5 + i)] = l

    copies = []
    for k in list(range(1, groups)) + [0]:
        peer = lax.rem(mine + k, groups)
        columns = pl.ds(pl.multiple_of(peer * part, 128), part)
        points = basis[:, columns]
        for b in range(slabs // 4):
            ag = dot(ahl[b], points)
            both = wg[b, :, columns] * (ag[: 4 * cols] + ag[4 * cols :])
            for i in range(4):
                esend[k, 4 * b + i : 4 * b + i + 1] = jnp.sum(
                    both[cols * i : cols * (i + 1)], axis=0, keepdims=True
                )
        esend[k, slabs : slabs + 8, 0:128] = ctot[...]
        if part > 128:
            esend[k, slabs : slabs + 8, 128:] = jnp.zeros((8, part - 128), F32)
        if k > 0:
            copies.append(
                pltpu.make_async_remote_copy(
                    src_ref=esend.at[k], dst_ref=erecv.at[k],
                    send_sem=es.at[k], recv_sem=er.at[k],
                    device_id=(peer, me), device_id_type=MESH,
                )
            )
            copies[-1].start()
    summed = esend[0]
    for k in range(1, groups):
        copies[k - 1].wait_recv()
        summed = summed + erecv[k]
    current = jnp.sum(summed[slabs : slabs + 8, 0:128])
    factor = (all_slabs * grid * (2.0 / small)) / current
    out[...] = summed[0:slabs] * factor
    for copy in copies:
        copy.wait_send()

    pair.wait_send()

    @pl.when(core == 1)
    def _():
        entry.wait_send()
        leaving.wait_send()
        for j in range(chips):
            @pl.when(j > chip)
            def _():
                offset_to(j).wait_send()

        @pl.when(inner)
        def _():
            for j in range(chips):
                @pl.when(j > chip)
                def _():
                    transfer_to(j, 1).wait_send()

                @pl.when(j < chip)
                def _():
                    transfer_to(j, 0).wait_send()

    @pl.when(core == 0)
    def _():
        joining.wait_send()
        for j in range(chips):
            @pl.when(j < chip)
            def _():
                exit_to(j).wait_send()


def local(wavefunction, injected_modes, factor_blocks, pivot_inverse, mode_velocity, energy_weight, mode_basis):
    n = lax.axis_size("slab")
    groups = lax.axis_size("energy")
    _, slabs, cols, modes = wavefunction.shape
    grid = mode_basis.shape[1]
    part = grid // groups
    vmem = pl.BlockSpec(memory_space=pltpu.VMEM)
    hbm = pl.BlockSpec(memory_space=pl.ANY)
    result = pl.pallas_call(
        functools.partial(kernel, n, groups),
        out_shape=jax.ShapeDtypeStruct((slabs, part), F32),
        in_specs=[vmem, vmem, hbm, hbm, vmem, vmem, vmem],
        out_specs=vmem,
        scratch_shapes=[
            pltpu.VMEM((slabs, modes, modes), F32),
            pltpu.VMEM((slabs, modes, modes), F32),
            pltpu.VMEM((slabs // 4, 8 * cols, modes), BF16),
            pltpu.SemaphoreType.DMA((slabs,)),
            pltpu.SemaphoreType.DMA,
            pltpu.VMEM((modes, modes), BF16),
            pltpu.VMEM((modes, modes), BF16),
            pltpu.VMEM((cols, modes), F32),
            pltpu.VMEM((cols, modes), F32),
            pltpu.VMEM((slabs, modes, modes), BF16),
            pltpu.VMEM((slabs, modes, modes), BF16),
            pltpu.VMEM((slabs, modes, modes), BF16),
            pltpu.VMEM((slabs, modes, modes), BF16),
            pltpu.VMEM((slabs, modes, modes), BF16),
            pltpu.VMEM((slabs, modes, modes), BF16),
            pltpu.VMEM((modes, modes), BF16),
            pltpu.VMEM((modes, modes), BF16),
            pltpu.VMEM((slabs, cols, modes), F32),
            pltpu.VMEM((slabs, cols, modes), F32),
            pltpu.VMEM((slabs, cols, modes), F32),
            pltpu.VMEM((slabs // 4, 4 * cols, grid), F32),
            pltpu.VMEM((2, modes + cols, modes), F32),
            pltpu.VMEM((cols, modes), F32),
            pltpu.VMEM((cols, modes), F32),
            pltpu.VMEM((8, 128), F32),
            pltpu.VMEM((8, 128), F32),
            pltpu.VMEM((modes + cols + 8, modes), F32),
            pltpu.VMEM((modes + cols + 8, modes), F32),
            pltpu.VMEM((cols + 8, modes), F32),
            pltpu.VMEM((n // 2, cols + 8, modes), F32),
            pltpu.VMEM((modes, modes), F32),
            pltpu.VMEM((n // 2, modes, modes), F32),
            pltpu.VMEM((cols + 8, modes), F32),
            pltpu.VMEM((cols + 8, modes), F32),
            pltpu.VMEM((cols, modes), F32),
            pltpu.VMEM((cols, modes), F32),
            pltpu.VMEM((cols + 8, modes), F32),
            pltpu.VMEM((n // 2, cols + 8, modes), F32),
            pltpu.VMEM((cols + 8, modes), F32),
            pltpu.VMEM((cols + 8, modes), F32),
            pltpu.VMEM((groups, slabs + 8, part), F32),
            pltpu.VMEM((groups, slabs + 8, part), F32),
            pltpu.SemaphoreType.DMA,
            pltpu.SemaphoreType.DMA,
            pltpu.SemaphoreType.DMA((n // 2,)),
            pltpu.SemaphoreType.DMA((n // 2,)),
            pltpu.SemaphoreType.DMA((n // 2,)),
            pltpu.SemaphoreType.DMA((n // 2,)),
            pltpu.SemaphoreType.DMA,
            pltpu.SemaphoreType.DMA,
            pltpu.SemaphoreType.DMA,
            pltpu.SemaphoreType.DMA,
            pltpu.SemaphoreType.DMA((n // 2,)),
            pltpu.SemaphoreType.DMA((n // 2,)),
            pltpu.SemaphoreType.DMA,
            pltpu.SemaphoreType.DMA,
            pltpu.SemaphoreType.DMA((groups,)),
            pltpu.SemaphoreType.DMA((groups,)),
        ],
        compiler_params=pltpu.CompilerParams(
            collective_id=0, has_side_effects=True, vmem_limit_bytes=60 * 1024 * 1024
        ),
    )(
        wavefunction[0],
        injected_modes,
        factor_blocks[0],
        pivot_inverse[0],
        mode_velocity,
        energy_weight.reshape(1, 1),
        mode_basis,
    )
    return result.T


def solution(mesh):
    return jax.shard_map(
        local,
        mesh=mesh,
        in_specs=(
            P("energy", "slab", None, None),
            P("energy", None),
            P("energy", "slab", None, None),
            P("energy", "slab", None, None),
            P("energy", None),
            P("energy"),
            P(),
        ),
        out_specs=P("energy", "slab"),
        check_vma=False,
    )
```

profile of v0, /device:TPU:0, one launch (start us, length us, event | category | flops | bytes accessed | tf_op | source)
XLA Modules:
  0.0 39.0 jit_solution(15580745780709056119)
XLA Ops:
  0.7 37.0 %shard_map.73 = f32[16,256]{1,0:T(8,128)} custom-call(bf16[16,64,256]{2,1,0:T(8,128)(2,1)} %bitcast.8, s32[1,64]{1,0:T(1,128)} %inj.1, f32[16,256,256]{2,1,0:T(8,128)} %bitcast.6, f32[16,256,256]{2,1,0:T(8,128)} %bitcast.7, f32[1,256]{1,0:T(1,128)} %vel.1, f32[1,1]{1,0:T(1,128)} %bitcast.5.ew, bf16[256,1024]{1,0:T(8,128)(2,1)} %basis.1), custom_call_target="tpu_custom_call" | custom-call | tf_op jit(solution)/shard_map/pallas_call | solution.py:419
  37.7 1.3 %copy.10 = f32[256,16]{0,1:T(8,128)} copy(f32[256,16]{0,1:T(8,128)} %bitcast.9) | data formatting | bytes 32768
where the time goes:
time: 39.4 us; the launch traced here: 39 us
  Pallas kernels  37 us (94%)
  local copies, waits for them, and re-layouts  1.32 us (3%)
  between operations  0.66 us (2%)
    pallas_call x1, Pallas kernels, local(): pl.pallas_call(functools.partial(kernel, n, groups), out_shape=jax.ShapeD...  37 us
    unnamed x1, local copies, waits for them, and re-layouts  1.32 us

commit v1 on v0

v1 whole, which is shorter than its diff:
```python
import functools
import jax
import jax.numpy as jnp
from jax import lax
from jax.experimental import pallas as pl
from jax.experimental.pallas import tpu as pltpu
from jax.sharding import PartitionSpec as P

F32 = jnp.float32
BF16 = jnp.bfloat16
MESH = pl.DeviceIdType.MESH


def split(x):
    hi = x.astype(BF16)
    return hi, (x - hi.astype(F32)).astype(BF16)


def dot(a, b, transposed=False):
    return lax.dot_general(
        a, b, (((1,), (1 if transposed else 0,)), ((), ())), preferred_element_type=F32
    )


def mm_split(ah, al, bh, bl, transposed=False):
    rows = ah.shape[0]
    both = dot(jnp.concatenate([ah, al], axis=0), bh, transposed)
    return both[:rows] + both[rows:] + dot(ah, bl, transposed)


def mm(a, bh, bl, transposed=False):
    ah, al = split(a)
    return mm_split(ah, al, bh, bl, transposed)


def kernel(
    n, groups,
    wave, inj, fac_hbm, piv_hbm, vel, ew, basis,
    out,
    fac, piv, ahl, fac_sem, piv_sem,
    fh, fl, uh, ul, vh, vl, th, tl, zh, zl, wh, wl, gh, gl, ch, cl, srh, srl,
    state, rest, adj, wg, off, scaled_ref, whole_off, chip_off, local_e, exit_own,
    inc, incb, cinc, cur,
    po_s, po_r, pu_s, pu_r, pg_s, pg_r, osend, orecv, tsend, trecv, urecv, csend, crecv,
    isend, irecv, ysend, yrecv, jsend, jrecv, zsend, zrecv, ssend, srecv, esend, erecv,
    pos, por, pus, pur, pgs, pgr, os, our, us, ur, ts, tr, cs, cr, is_, ir, ys, yr, js, jr,
    zs, zr, ss, sr, es, er,
):
    me = lax.axis_index("slab")
    mine = lax.axis_index("energy")
    slabs, cols, modes = wave.shape
    grid = basis.shape[1]
    part = grid // groups
    chips = n // 2
    chip = me // 2
    core = lax.rem(me, 2)
    other = me + 1 - 2 * core
    odd = lax.rem(chip, 2)
    half = slabs // 2
    all_slabs = n * slabs
    small = 2.0 / (all_slabs * cols * modes * groups * 4096.0)

    def factor_in(s):
        return pltpu.make_async_copy(fac_hbm.at[s], fac.at[s], fac_sem.at[s])

    for i in range(half // 2):
        for k in range(2):
            factor_in(k * half + i).start()
            factor_in(k * half + half - 1 - i).start()
    pivots_in = pltpu.make_async_copy(piv_hbm, piv, piv_sem)
    pivots_in.start()

    barrier = pltpu.get_barrier_semaphore()

    for k in range(1, n):
        pl.semaphore_signal(
            barrier, inc=1, device_id=(mine, lax.rem(me + k, n)), device_id_type=MESH
        )
    for k in range(1, groups):
        peer = lax.rem(mine + k, groups)
        pl.semaphore_signal(barrier, inc=1, device_id=(peer, me), device_id_type=MESH)

    rows_at = lax.broadcasted_iota(jnp.int32, (cols, cols), 0)
    cols_at = lax.broadcasted_iota(jnp.int32, (cols, cols), 1)
    picked = jnp.sum(
        jnp.where(rows_at == cols_at, jnp.broadcast_to(inj[...].astype(F32), (cols, cols)), 0.0),
        axis=1, keepdims=True,
    )
    mode_at = lax.broadcasted_iota(jnp.int32, (cols, modes), 1).astype(F32)
    velocity = jnp.broadcast_to(vel[...], (cols, modes))
    at_injected = jnp.sum(jnp.where(mode_at == picked, velocity, 0.0), axis=1, keepdims=True)
    scaled_ref[...] = ew[...] * (1.0 / at_injected) * velocity

    eye = (
        lax.broadcasted_iota(jnp.int32, (modes, modes), 0)
        == lax.broadcasted_iota(jnp.int32, (modes, modes), 1)
    ).astype(F32).astype(BF16)

    for k in range(2):
        ch[k] = eye
        cl[k] = jnp.zeros((modes, modes), BF16)
        off[k] = jnp.zeros((cols, modes), F32)
    cur[...] = jnp.zeros_like(cur)

    def chain(i, carry):
        moved = []
        for k in range(2):
            s = k * half + i
            w = wave[s].astype(F32)
            sw = scaled_ref[...] * w
            sq = sw * w
            part_sum = sq[0:8]
            for j in range(1, cols // 8):
                part_sum = part_sum + sq[8 * j : 8 * j + 8]
            tile = part_sum[:, 0:128]
            for j in range(1, modes // 128):
                tile = tile + part_sum[:, 128 * j : 128 * j + 128]
            cur[...] += tile
            source = sw * small
            h, l = split(source)
            srh[s] = h
            srl[s] = l
            own = off[k] + source
            state[s] = own
            back = k * half + half - 1 - i
            moved.append(mm_split(ch[k], cl[k], fh[back], fl[back], True))
            moved.append(mm(own, fh[s], fl[s]))
        for k in range(2):
            back = k * half + half - 1 - i
            h, l = split(moved[2 * k])
            ch[k] = h
            cl[k] = l
            uh[back] = h
            ul[back] = l
            off[k] = moved[2 * k + 1]
        return carry

    def chain_in(i, carry):
        for k in range(2):
            for s in (k * half + i, k * half + half - 1 - i):
                factor_in(s).wait()
                h, l = split(fac[s])
                fh[s] = h
                fl[s] = l
        return chain(i, carry)

    lax.fori_loop(0, half // 2, chain_in, 0, unroll=2)
    lax.fori_loop(half // 2, half, chain, 0, unroll=2)

    def copy_to(source, target, send, receive, device):
        return pltpu.make_async_remote_copy(
            src_ref=source, dst_ref=target, send_sem=send, recv_sem=receive,
            device_id=(mine, device), device_id_type=MESH,
        )

    pair_off = copy_to(po_s, po_r, pos, por, other)
    pair_u = copy_to(pu_s, pu_r, pus, pur, other)
    pair_g = copy_to(pg_s, pg_r, pgs, pgr, other)
    entry = copy_to(isend, irecv, is_, ir, other)
    joining = copy_to(jsend, jrecv, js, jr, other)

    def chip_at(j):
        return 2 * lax.rem(j, chips) + 1

    offset_on = copy_to(osend, orecv, os, our, chip_at(chip + 1))
    transfer_on = copy_to(tsend, urecv, us, ur, chip_at(chip + 1))

    def carried_to(k):
        return copy_to(csend, crecv, cs.at[k], cr, chip_at(chip + 1 + k))

    def transfer_to(j):
        return copy_to(tsend, trecv.at[chip], ts.at[j], tr.at[chip], 2 * j + 1)

    def exit_to(j):
        return copy_to(ysend, yrecv.at[chip], ys.at[j], yr.at[chip], 2 * j + 1)

    def wait_transfer(j):
        copy_to(tsend, trecv.at[j], ts.at[j], tr.at[j], other).wait_recv()

    def wait_exit(j):
        copy_to(ysend, yrecv.at[j], ys.at[j], yr.at[j], other).wait_recv()

    def tile_to(k):
        peer = lax.rem(mine + k, groups)
        return pltpu.make_async_remote_copy(
            src_ref=zsend, dst_ref=zrecv.at[k], send_sem=zs.at[k], recv_sem=zr.at[k],
            device_id=(peer, me), device_id_type=MESH,
        )

    def share_to(d):
        return copy_to(ssend, srecv.at[chip], ss.at[d], sr.at[chip], d)

    inner = jnp.logical_and(chip > 0, chip < chips - 1)
    onward = jnp.logical_and(odd == 0, chip < chips - 1)

    off_a = off[0]
    whole_off[...] = mm(off_a, uh[half], ul[half], True) + off[1]
    po_s[0:cols] = whole_off[...]
    po_s[cols:, 0:128] = cur[...]
    po_s[cols:, 128:] = jnp.zeros((8, modes - 128), F32)

    pl.semaphore_wait(barrier, n + groups - 2)

    @pl.when(core == 0)
    def _():
        pair_off.start()

    whole = mm_split(uh[half], ul[half], uh[0], ul[0])
    h, l = split(whole)
    th[...] = h
    tl[...] = l

    @pl.when(core == 0)
    def _():
        pu_s[...] = whole
        pair_u.start()

    @pl.when(core == 1)
    def _():
        pair_off.wait_recv()
        chip_off[...] = mm(po_r[0:cols], th[...], tl[...], True) + whole_off[...]

        @pl.when(onward)
        def _():
            osend[...] = chip_off[...]
            offset_on.start()

        zsend[...] = cur[...] + po_r[cols:, 0:128]
        for k in range(1, groups):
            tile_to(k).start()
        pair_u.wait_recv()
        h, l = split(pu_r[...])
        zh[...] = h
        zl[...] = l
        joined = mm_split(th[...], tl[...], h, l)
        tsend[...] = joined

        @pl.when(jnp.logical_and(onward, chip > 0))
        def _():
            transfer_on.start()

        h, l = split(joined)
        wh[...] = h
        wl[...] = l

    pivots_in.wait()
    for k in range(2):
        end = k * half + half - 1
        h, l = split(piv[end])
        vh[end] = h
        vl[end] = l
        rest[end] = jnp.zeros((cols, modes), F32)

    def climb(i, carry):
        firsts = []
        for k in range(2):
            s = k * half + half - 2 - i
            first = mm_split(
                jnp.concatenate([fh[s], srh[s + 1]], axis=0),
                jnp.concatenate([fl[s], srl[s + 1]], axis=0),
                vh[s + 1], vl[s + 1],
            )
            firsts.append(jnp.concatenate([first[0:modes], first[modes:] + rest[s + 1]], axis=0))
        seconds = []
        for k in range(2):
            s = k * half + half - 2 - i
            seconds.append(mm(firsts[k], fh[s], fl[s], True))
        for k in range(2):
            s = k * half + half - 2 - i
            h, l = split(piv[s] + seconds[k][0:modes])
            vh[s] = h
            vl[s] = l
            rest[s] = seconds[k][modes:]
        return carry

    early = (half - 1) // 2
    lax.fori_loop(0, early, climb, 0)

    def carry_on():
        csend[...] = mm(cinc[...], wh[...], wl[...], True) + chip_off[...]
        carried_to(0).start()

        @pl.when(chip < chips - 2)
        def _():
            carried_to(1).start()

    cinc[...] = jnp.zeros_like(cinc)

    @pl.when(core == 1)
    def _():
        @pl.when(chip == 1)
        def _():
            offset_on.wait_recv()
            cinc[...] = orecv[...]
            if chips > 2:
                carry_on()

        @pl.when(inner)
        def _():
            for j in range(chips):
                @pl.when(j < chip)
                def _():
                    transfer_to(j).start()

    lax.fori_loop(early, half - 1, climb, 0)

    lead_h = dot(eye, uh[0], True).astype(BF16)
    lead_l = dot(eye, ul[0], True).astype(BF16)
    row_h, row_l = split(state[half] + off_a)
    first = mm_split(
        jnp.concatenate([lead_h, row_h], axis=0),
        jnp.concatenate([lead_l, row_l], axis=0),
        vh[half], vl[half],
    )
    first = jnp.concatenate([first[0:modes], first[modes:] + rest[half]], axis=0)
    second = mm(first, uh[0], ul[0])
    own_g = second[0:modes] + vh[0].astype(F32) + vl[0].astype(F32)
    own_e = second[modes:] + rest[0] + mm_split(srh[0], srl[0], vh[0], vl[0])

    @pl.when(core == 0)
    def _():
        pg_s[0:modes] = own_g
        pg_s[modes:] = own_e
        pair_g.start()
        entry.wait_recv()
        inc[...] = irecv[...]

    @pl.when(core == 1)
    def _():
        h, l = split(own_g)
        gh[...] = h
        gl[...] = l
        local_e[...] = own_e

        @pl.when(chip > 1)
        def _():
            carried_to(0).wait_recv()
            cinc[...] = crecv[...]

            @pl.when(odd == 1)
            def _():
                offset_on.wait_recv()
                transfer_on.wait_recv()
                h, l = split(urecv[...])
                cinc[...] = mm(cinc[...], h, l, True) + orecv[...]

                @pl.when(chip < chips - 1)
                def _():
                    carry_on()

        isend[...] = cinc[...]
        entry.start()
        inc[...] = mm(cinc[...], zh[...], zl[...], True) + po_r[0:cols]
        exit_own[...] = local_e[...] + mm(inc[...], gh[...], gl[...])
        pair_g.wait_recv()

        @pl.when(chip > 0)
        def _():
            h, l = split(pg_r[0:modes])
            ysend[...] = (
                pg_r[modes:] + mm(cinc[...], h, l) + mm(exit_own[...], zh[...], zl[...])
            )
            for j in range(chips):
                @pl.when(j < chip)
                def _():
                    exit_to(j).start()

    incb[...] = mm(inc[...], uh[0], ul[0], True) + off_a

    def settle(i, moving):
        following = []
        for k in range(2):
            s = k * half + i
            h, l = split(moving[k])
            adj[s] = rest[s] + mm(state[s] + moving[k], vh[s], vl[s])
            following.append(mm_split(h, l, fh[s], fl[s]))
        return tuple(following)

    lax.fori_loop(0, half, settle, (inc[...], incb[...]), unroll=2)

    def waves(b, carry):
        wg[b] = dot(wave[pl.ds(4 * b, 4)].reshape(4 * cols, modes), basis[...])
        return carry

    lax.fori_loop(0, slabs // 4, waves, 0)

    @pl.when(core == 1)
    def _():
        tiles = zsend[...]
        for k in range(1, groups):
            tile_to(k).wait_recv()
            tiles = tiles + zrecv[k]
        ssend[...] = tiles
        for d in range(n):
            @pl.when(me != d)
            def _():
                share_to(d).start()

        inc[...] = jnp.zeros_like(inc)
        for j in range(chips - 1, 0, -1):
            @pl.when(chip < j)
            def _():
                if j < chips - 1:
                    wait_transfer(j)
                wait_exit(j)
                if j == chips - 1:
                    inc[...] = yrecv[j]
                else:
                    h, l = split(trecv[j])
                    inc[...] = mm(inc[...], h, l) + yrecv[j]

        jsend[...] = exit_own[...] + mm(inc[...], th[...], tl[...])
        joining.start()

    @pl.when(core == 0)
    def _():
        joining.wait_recv()
        inc[...] = jrecv[...]

    incb[...] = adj[half] + mm(inc[...], uh[half], ul[half])

    for b in range(slabs // 4):
        for i in range(4):
            s = 4 * b + i
            entering = incb if s < half else inc
            h, l = split(adj[s] + mm(entering[...], uh[s], ul[s]))
            ahl[b, cols * i : cols * (i + 1)] = h
            ahl[b, cols * (4 + i) : cols * (5 + i)] = l

    def products(slot, peer):
        columns = pl.ds(pl.multiple_of(peer * part, 128), part)
        points = basis[:, columns]
        for b in range(slabs // 4):
            ag = dot(ahl[b], points)
            both = wg[b, :, columns] * (ag[: 4 * cols] + ag[4 * cols :])
            for i in range(4):
                esend[slot, 4 * b + i : 4 * b + i + 1] = jnp.sum(
                    both[cols * i : cols * (i + 1)], axis=0, keepdims=True
                )

    copies = []
    low = 0
    high = groups - 1
    for slot in range(groups - 1):
        above = (high - mine >= mine - low).astype(jnp.int32)
        peer = above * high + (1 - above) * low
        low = low + 1 - above
        high = high - above
        products(slot, peer)
        at = lax.rem(peer + groups - mine, groups)
        copies.append(
            pltpu.make_async_remote_copy(
                src_ref=esend.at[slot], dst_ref=erecv.at[at],
                send_sem=es.at[slot], recv_sem=er.at[at],
                device_id=(peer, me), device_id_type=MESH,
            )
        )
        copies[-1].start()
    products(groups - 1, mine)

    @pl.when(core == 0)
    def _():
        cur[...] = jnp.zeros_like(cur)

    @pl.when(core == 1)
    def _():
        cur[...] = ssend[...]

    for j in range(chips):
        @pl.when(me != 2 * j + 1)
        def _():
            copy_to(ssend, srecv.at[j], ss.at[0], sr.at[j], other).wait_recv()
            cur[...] += srecv[j]

    current = jnp.sum(cur[...])
    factor = (all_slabs * grid * (2.0 / small)) / current
    summed = esend[groups - 1]
    for k in range(1, groups):
        pltpu.make_async_remote_copy(
            src_ref=esend.at[0], dst_ref=erecv.at[k], send_sem=es.at[0], recv_sem=er.at[k],
            device_id=(mine, other), device_id_type=MESH,
        ).wait_recv()
        summed = summed + erecv[k]
    out[...] = summed * factor
    for copy in copies:
        copy.wait_send()

    @pl.when(core == 0)
    def _():
        pair_off.wait_send()
        pair_u.wait_send()
        pair_g.wait_send()

    @pl.when(core == 1)
    def _():
        entry.wait_send()
        joining.wait_send()
        for k in range(1, groups):
            tile_to(k).wait_send()
        for d in range(n):
            @pl.when(me != d)
            def _():
                share_to(d).wait_send()

        @pl.when(onward)
        def _():
            offset_on.wait_send()

        @pl.when(jnp.logical_and(onward, chip > 0))
        def _():
            transfer_on.wait_send()

        @pl.when(jnp.logical_and(odd == 1, chip < chips - 1))
        def _():
            carried_to(0).wait_send()

            @pl.when(chip < chips - 2)
            def _():
                carried_to(1).wait_send()

        @pl.when(inner)
        def _():
            for j in range(chips):
                @pl.when(j < chip)
                def _():
                    transfer_to(j).wait_send()

        @pl.when(chip > 0)
        def _():
            for j in range(chips):
                @pl.when(j < chip)
                def _():
                    exit_to(j).wait_send()


def local(wavefunction, injected_modes, factor_blocks, pivot_inverse, mode_velocity, energy_weight, mode_basis):
    n = lax.axis_size("slab")
    groups = lax.axis_size("energy")
    _, slabs, cols, modes = wavefunction.shape
    grid = mode_basis.shape[1]
    part = grid // groups
    chips = n // 2
    vmem = pl.BlockSpec(memory_space=pltpu.VMEM)
    hbm = pl.BlockSpec(memory_space=pl.ANY)
    dma = pltpu.SemaphoreType.DMA

    def full(*shape):
        return pltpu.VMEM(shape, F32)

    def short(*shape):
        return pltpu.VMEM(shape, BF16)

    result = pl.pallas_call(
        functools.partial(kernel, n, groups),
        out_shape=jax.ShapeDtypeStruct((slabs, part), F32),
        in_specs=[vmem, vmem, hbm, hbm, vmem, vmem, vmem],
        out_specs=vmem,
        scratch_shapes=[
            full(slabs, modes, modes),
            full(slabs, modes, modes),
            short(slabs // 4, 8 * cols, modes),
            dma((slabs,)),
            dma,
        ]
        + [short(slabs, modes, modes)] * 6
        + [short(modes, modes)] * 8
        + [short(2, modes, modes)] * 2
        + [short(slabs, cols, modes)] * 2
        + [full(slabs, cols, modes)] * 3
        + [
            full(slabs // 4, 4 * cols, grid),
            full(2, cols, modes),
        ]
        + [full(cols, modes)] * 5
        + [full(cols, modes)] * 3
        + [full(8, 128)]
        + [full(cols + 8, modes)] * 2
        + [full(modes, modes)] * 2
        + [full(modes + cols, modes)] * 2
        + [full(cols, modes)] * 2
        + [
            full(modes, modes),
            full(chips, modes, modes),
            full(modes, modes),
        ]
        + [full(cols, modes)] * 2
        + [full(cols, modes)] * 2
        + [full(cols, modes), full(chips, cols, modes)]
        + [full(cols, modes)] * 2
        + [full(8, 128), full(groups, 8, 128)]
        + [full(8, 128), full(chips, 8, 128)]
        + [full(groups, slabs, part)] * 2
        + [dma] * 6
        + [dma] * 4
        + [dma((chips,))] * 2
        + [dma((2,)), dma]
        + [dma] * 2
        + [dma((chips,))] * 2
        + [dma] * 2
        + [dma((groups,))] * 2
        + [dma((n,)), dma((chips,))]
        + [dma((groups,))] * 2,
        compiler_params=pltpu.CompilerParams(
            collective_id=0, has_side_effects=True, vmem_limit_bytes=60 * 1024 * 1024
        ),
    )(
        wavefunction[0],
        injected_modes,
        factor_blocks[0],
        pivot_inverse[0],
        mode_velocity,
        energy_weight.reshape(1, 1),
        mode_basis,
    )
    return result.T


def solution(mesh):
    return jax.shard_map(
        local,
        mesh=mesh,
        in_specs=(
            P("energy", "slab", None, None),
            P("energy", None),
            P("energy", "slab", None, None),
            P("energy", "slab", None, None),
            P("energy", None),
            P("energy"),
            P(),
        ),
        out_specs=P("energy", "slab"),
        check_vma=False,
    )
```

time: 39.4 us -> 33 us (0.84)
  Pallas kernels: 37 us -> 30.8 us
    pallas_call x1, Pallas kernels: 37 us -> 30.8 us  [local(): pl.pallas_call(functools.partial(kernel, n, groups), out_shape=jax.ShapeD...]
where the time goes in v1:
time: 33 us; the launch traced here: 32.7 us
  Pallas kernels  30.8 us (93%)
  local copies, waits for them, and re-layouts  1.32 us (4%)
  between operations  0.66 us (2%)
    pallas_call x1, Pallas kernels, local(): pl.pallas_call(functools.partial(kernel, n, groups), out_shape=jax.ShapeD...  30.8 us
    unnamed x1, local copies, waits for them, and re-layouts  1.32 us

profile of v1, /device:TPU:0, one launch (start us, length us, event | category | flops | bytes accessed | tf_op | source)
XLA Modules:
  0.0 32.7 jit_solution(11649440454668587190)
XLA Ops:
  0.7 30.8 %shard_map.73 = f32[16,256]{1,0:T(8,128)} custom-call(bf16[16,64,256]{2,1,0:T(8,128)(2,1)} %bitcast.8, s32[1,64]{1,0:T(1,128)} %inj.1, f32[16,256,256]{2,1,0:T(8,128)} %bitcast.6, f32[16,256,256]{2,1,0:T(8,128)} %bitcast.7, f32[1,256]{1,0:T(1,128)} %vel.1, f32[1,1]{1,0:T(1,128)} %bitcast.5.ew, bf16[256,1024]{1,0:T(8,128)(2,1)} %basis.1), custom_call_target="tpu_custom_call" | custom-call | tf_op jit(solution)/shard_map/pallas_call | solution.py:553
  31.4 1.3 %copy.10 = f32[256,16]{0,1:T(8,128)} copy(f32[256,16]{0,1:T(8,128)} %bitcast.9) | data formatting | bytes 32768

commit v2 on v1

--- a/solution.py
+++ b/solution.py
@@ -38,8 +38,8 @@
     wave, inj, fac_hbm, piv_hbm, vel, ew, basis,
     out,
     fac, piv, ahl, fac_sem, piv_sem,
-    fh, fl, uh, ul, vh, vl, th, tl, zh, zl, wh, wl, gh, gl, ch, cl, srh, srl,
-    state, rest, adj, wg, off, scaled_ref, whole_off, chip_off, local_e, exit_own,
+    fh, fl, uh, ul, vh, vl, xh, xl, th, tl, zh, zl, wh, wl, gh, gl, srh, srl,
+    rest, adj, wg, off, scaled_ref, whole_off, chip_off, local_e, exit_own,
     inc, incb, cinc, cur,
     po_s, po_r, pu_s, pu_r, pg_s, pg_r, osend, orecv, tsend, trecv, urecv, csend, crecv,
     isend, irecv, ysend, yrecv, jsend, jrecv, zsend, zrecv, ssend, srecv, esend, erecv,
@@ -63,9 +63,8 @@
     def factor_in(s):
         return pltpu.make_async_copy(fac_hbm.at[s], fac.at[s], fac_sem.at[s])
 
-    for i in range(half // 2):
-        for k in range(2):
-            factor_in(k * half + i).start()
+    for i in range(half):
+        for k in range(2):
             factor_in(k * half + half - 1 - i).start()
     pivots_in = pltpu.make_async_copy(piv_hbm, piv, piv_sem)
     pivots_in.start()
@@ -91,61 +90,89 @@
     at_injected = jnp.sum(jnp.where(mode_at == picked, velocity, 0.0), axis=1, keepdims=True)
     scaled_ref[...] = ew[...] * (1.0 / at_injected) * velocity
 
-    eye = (
-        lax.broadcasted_iota(jnp.int32, (modes, modes), 0)
-        == lax.broadcasted_iota(jnp.int32, (modes, modes), 1)
-    ).astype(F32).astype(BF16)
+    cur[...] = jnp.zeros_like(cur)
+
+    def bring(s):
+        w = wave[s].astype(F32)
+        sw = scaled_ref[...] * w
+        sq = sw * w
+        part_sum = sq[0:8]
+        for j in range(1, cols // 8):
+            part_sum = part_sum + sq[8 * j : 8 * j + 8]
+        tile = part_sum[:, 0:128]
+        for j in range(1, modes // 128):
+            tile = tile + part_sum[:, 128 * j : 128 * j + 128]
+        cur[...] += tile
+        h, l = split(sw * small)
+        srh[s] = h
+        srl[s] = l
+        factor_in(s).wait()
+        h, l = split(fac[s])
+        fh[s] = h
+        fl[s] = l
+        return h, l
 
     for k in range(2):
-        ch[k] = eye
-        cl[k] = jnp.zeros((modes, modes), BF16)
+        end = k * half + half - 1
+        h, l = bring(end)
+        uh[end] = h
+        ul[end] = l
         off[k] = jnp.zeros((cols, modes), F32)
-    cur[...] = jnp.zeros_like(cur)
+
+    def extended(s, h, l, bh, bl):
+        return mm_split(
+            jnp.concatenate([h, srh[s + 1]], axis=0), jnp.concatenate([l, srl[s + 1]], axis=0), bh, bl
+        )
 
     def chain(i, carry):
+        blocks = [bring(k * half + half - 2 - i) for k in range(2)]
         moved = []
         for k in range(2):
-            s = k * half + i
-            w = wave[s].astype(F32)
-            sw = scaled_ref[...] * w
-            sq = sw * w
-            part_sum = sq[0:8]
-            for j in range(1, cols // 8):
-                part_sum = part_sum + sq[8 * j : 8 * j + 8]
-            tile = part_sum[:, 0:128]
-            for j in range(1, modes // 128):
-                tile = tile + part_sum[:, 128 * j : 128 * j + 128]
-            cur[...] += tile
-            source = sw * small
-            h, l = split(source)
-            srh[s] = h
-            srl[s] = l
-            own = off[k] + source
-            state[s] = own
-            back = k * half + half - 1 - i
-            moved.append(mm_split(ch[k], cl[k], fh[back], fl[back], True))
-            moved.append(mm(own, fh[s], fl[s]))
-        for k in range(2):
-            back = k * half + half - 1 - i
-            h, l = split(moved[2 * k])
-            ch[k] = h
-            cl[k] = l
-            uh[back] = h
-            ul[back] = l
-            off[k] = moved[2 * k + 1]
+            s = k * half + half - 2 - i
+            h, l = blocks[k]
+            moved.append(extended(s, h, l, uh[s + 1], ul[s + 1]))
+        for k in range(2):
+            s = k * half + half - 2 - i
+            h, l = split(moved[k][0:modes])
+            uh[s] = h
+            ul[s] = l
+            off[k] += moved[k][modes:]
         return carry
 
-    def chain_in(i, carry):
-        for k in range(2):
-            for s in (k * half + i, k * half + half - 1 - i):
-                factor_in(s).wait()
-                h, l = split(fac[s])
-                fh[s] = h
-                fl[s] = l
-        return chain(i, carry)
-
-    lax.fori_loop(0, half // 2, chain_in, 0, unroll=2)
-    lax.fori_loop(half // 2, half, chain, 0, unroll=2)
+    def settle_ends():
+        pivots_in.wait()
+        for k in range(2):
+            end = k * half + half - 1
+            h, l = split(piv[end])
+            vh[end] = h
+            vl[end] = l
+            rest[end] = jnp.zeros((cols, modes), F32)
+
+    def climb(i, carry):
+        firsts = []
+        for k in range(2):
+            s = k * half + half - 2 - i
+            first = extended(s, fh[s], fl[s], vh[s + 1], vl[s + 1])
+            firsts.append(jnp.concatenate([first[0:modes], first[modes:] + rest[s + 1]], axis=0))
+        seconds = []
+        for k in range(2):
+            s = k * half + half - 2 - i
+            seconds.append(mm(firsts[k], fh[s], fl[s], True))
+        for k in range(2):
+            s = k * half + half - 2 - i
+            h, l = split(piv[s] + seconds[k][0:modes])
+            vh[s] = h
+            vl[s] = l
+            rest[s] = seconds[k][modes:]
+        return carry
+
+    beside = (half - 1) // 2 + -1
+    for i in range(half - 1):
+        chain(i, 0)
+        if i == half - 2 - beside:
+            settle_ends()
+        elif i > half - 2 - beside:
+            climb(i - (half - 1 - beside), 0)
 
     def copy_to(source, target, send, receive, device):
         return pltpu.make_async_remote_copy(
@@ -193,8 +220,10 @@
     inner = jnp.logical_and(chip > 0, chip < chips - 1)
     onward = jnp.logical_and(odd == 0, chip < chips - 1)
 
+    off[0] += mm_split(srh[0], srl[0], uh[0], ul[0])
     off_a = off[0]
-    whole_off[...] = mm(off_a, uh[half], ul[half], True) + off[1]
+    off_b = off[1] + mm_split(srh[half], srl[half], uh[half], ul[half])
+    whole_off[...] = mm(off_a, uh[half], ul[half]) + off_b
     po_s[0:cols] = whole_off[...]
     po_s[cols:, 0:128] = cur[...]
     po_s[cols:, 128:] = jnp.zeros((8, modes - 128), F32)
@@ -205,7 +234,7 @@
     def _():
         pair_off.start()
 
-    whole = mm_split(uh[half], ul[half], uh[0], ul[0])
+    whole = mm_split(uh[0], ul[0], uh[half], ul[half])
     h, l = split(whole)
     th[...] = h
     tl[...] = l
@@ -218,7 +247,7 @@
     @pl.when(core == 1)
     def _():
         pair_off.wait_recv()
-        chip_off[...] = mm(po_r[0:cols], th[...], tl[...], True) + whole_off[...]
+        chip_off[...] = mm(po_r[0:cols], th[...], tl[...]) + whole_off[...]
 
         @pl.when(onward)
         def _():
@@ -232,7 +261,7 @@
         h, l = split(pu_r[...])
         zh[...] = h
         zl[...] = l
-        joined = mm_split(th[...], tl[...], h, l)
+        joined = mm_split(h, l, th[...], tl[...])
         tsend[...] = joined
 
         @pl.when(jnp.logical_and(onward, chip > 0))
@@ -243,41 +272,12 @@
         wh[...] = h
         wl[...] = l
 
-    pivots_in.wait()
-    for k in range(2):
-        end = k * half + half - 1
-        h, l = split(piv[end])
-        vh[end] = h
-        vl[end] = l
-        rest[end] = jnp.zeros((cols, modes), F32)
-
-    def climb(i, carry):
-        firsts = []
-        for k in range(2):
-            s = k * half + half - 2 - i
-            first = mm_split(
-                jnp.concatenate([fh[s], srh[s + 1]], axis=0),
-                jnp.concatenate([fl[s], srl[s + 1]], axis=0),
-                vh[s + 1], vl[s + 1],
-            )
-            firsts.append(jnp.concatenate([first[0:modes], first[modes:] + rest[s + 1]], axis=0))
-        seconds = []
-        for k in range(2):
-            s = k * half + half - 2 - i
-            seconds.append(mm(firsts[k], fh[s], fl[s], True))
-        for k in range(2):
-            s = k * half + half - 2 - i
-            h, l = split(piv[s] + seconds[k][0:modes])
-            vh[s] = h
-            vl[s] = l
-            rest[s] = seconds[k][modes:]
-        return carry
-
-    early = (half - 1) // 2
-    lax.fori_loop(0, early, climb, 0)
+    early = min(beside + 2, half - 1)
+    for i in range(beside, early):
+        climb(i, 0)
 
     def carry_on():
-        csend[...] = mm(cinc[...], wh[...], wl[...], True) + chip_off[...]
+        csend[...] = mm(cinc[...], wh[...], wl[...]) + chip_off[...]
         carried_to(0).start()
 
         @pl.when(chip < chips - 2)
@@ -302,18 +302,17 @@
                 def _():
                     transfer_to(j).start()
 
-    lax.fori_loop(early, half - 1, climb, 0)
-
-    lead_h = dot(eye, uh[0], True).astype(BF16)
-    lead_l = dot(eye, ul[0], True).astype(BF16)
-    row_h, row_l = split(state[half] + off_a)
+    for i in range(early, half - 1):
+        climb(i, 0)
+
+    row_h, row_l = split(srh[half].astype(F32) + srl[half].astype(F32) + off_a)
     first = mm_split(
-        jnp.concatenate([lead_h, row_h], axis=0),
-        jnp.concatenate([lead_l, row_l], axis=0),
+        jnp.concatenate([uh[0], row_h], axis=0),
+        jnp.concatenate([ul[0], row_l], axis=0),
         vh[half], vl[half],
     )
     first = jnp.concatenate([first[0:modes], first[modes:] + rest[half]], axis=0)
-    second = mm(first, uh[0], ul[0])
+    second = mm(first, uh[0], ul[0], True)
     own_g = second[0:modes] + vh[0].astype(F32) + vl[0].astype(F32)
     own_e = second[modes:] + rest[0] + mm_split(srh[0], srl[0], vh[0], vl[0])
 
@@ -342,7 +341,7 @@
                 offset_on.wait_recv()
                 transfer_on.wait_recv()
                 h, l = split(urecv[...])
-                cinc[...] = mm(cinc[...], h, l, True) + orecv[...]
+                cinc[...] = mm(cinc[...], h, l) + orecv[...]
 
                 @pl.when(chip < chips - 1)
                 def _():
@@ -350,7 +349,7 @@
 
         isend[...] = cinc[...]
         entry.start()
-        inc[...] = mm(cinc[...], zh[...], zl[...], True) + po_r[0:cols]
+        inc[...] = mm(cinc[...], zh[...], zl[...]) + po_r[0:cols]
         exit_own[...] = local_e[...] + mm(inc[...], gh[...], gl[...])
         pair_g.wait_recv()
 
@@ -358,22 +357,24 @@
         def _():
             h, l = split(pg_r[0:modes])
             ysend[...] = (
-                pg_r[modes:] + mm(cinc[...], h, l) + mm(exit_own[...], zh[...], zl[...])
+                pg_r[modes:] + mm(cinc[...], h, l) + mm(exit_own[...], zh[...], zl[...], True)
             )
             for j in range(chips):
                 @pl.when(j < chip)
                 def _():
                     exit_to(j).start()
 
-    incb[...] = mm(inc[...], uh[0], ul[0], True) + off_a
+    incb[...] = mm(inc[...], uh[0], ul[0]) + off_a
 
     def settle(i, moving):
         following = []
         for k in range(2):
             s = k * half + i
-            h, l = split(moving[k])
-            adj[s] = rest[s] + mm(state[s] + moving[k], vh[s], vl[s])
+            h, l = split(moving[k] + (srh[s].astype(F32) + srl[s].astype(F32)))
+            adj[s] = rest[s] + mm_split(h, l, vh[s], vl[s])
             following.append(mm_split(h, l, fh[s], fl[s]))
+            xh[s] = uh[s].T
+            xl[s] = ul[s].T
         return tuple(following)
 
     lax.fori_loop(0, half, settle, (inc[...], incb[...]), unroll=2)
@@ -407,9 +408,9 @@
                     inc[...] = yrecv[j]
                 else:
                     h, l = split(trecv[j])
-                    inc[...] = mm(inc[...], h, l) + yrecv[j]
-
-        jsend[...] = exit_own[...] + mm(inc[...], th[...], tl[...])
+                    inc[...] = mm(inc[...], h, l, True) + yrecv[j]
+
+        jsend[...] = exit_own[...] + mm(inc[...], th[...], tl[...], True)
         joining.start()
 
     @pl.when(core == 0)
@@ -417,13 +418,13 @@
         joining.wait_recv()
         inc[...] = jrecv[...]
 
-    incb[...] = adj[half] + mm(inc[...], uh[half], ul[half])
+    incb[...] = adj[half] + mm(inc[...], xh[half], xl[half])
 
     for b in range(slabs // 4):
         for i in range(4):
             s = 4 * b + i
             entering = incb if s < half else inc
-            h, l = split(adj[s] + mm(entering[...], uh[s], ul[s]))
+            h, l = split(adj[s] + mm(entering[...], xh[s], xl[s]))
             ahl[b, cols * i : cols * (i + 1)] = h
             ahl[b, cols * (4 + i) : cols * (5 + i)] = l
 
@@ -562,11 +563,10 @@
             dma((slabs,)),
             dma,
         ]
-        + [short(slabs, modes, modes)] * 6
+        + [short(slabs, modes, modes)] * 8
         + [short(modes, modes)] * 8
-        + [short(2, modes, modes)] * 2
         + [short(slabs, cols, modes)] * 2
-        + [full(slabs, cols, modes)] * 3
+        + [full(slabs, cols, modes)] * 2
         + [
             full(slabs // 4, 4 * cols, grid),
             full(2, cols, modes),

time: 33 us -> 31.7 us (0.961)
  Pallas kernels: 30.8 us -> 29.4 us
    pallas_call x1, Pallas kernels: 30.8 us -> 29.4 us  [local(): pl.pallas_call(functools.partial(kernel, n, groups), out_shape=jax.ShapeD...]
where the time goes in v2:
time: 31.7 us; the launch traced here: 31.4 us
  Pallas kernels  29.4 us (93%)
  local copies, waits for them, and re-layouts  1.32 us (4%)
  between operations  0.66 us (2%)
    pallas_call x1, Pallas kernels, local(): pl.pallas_call(functools.partial(kernel, n, groups), out_shape=jax.ShapeD...  29.4 us
    unnamed x1, local copies, waits for them, and re-layouts  1.32 us

profile of v2, /device:TPU:0, one launch (start us, length us, event | category | flops | bytes accessed | tf_op | source)
XLA Modules:
  0.0 31.4 jit_solution(14257760055149246671)
XLA Ops:
  0.7 29.4 %shard_map.73 = f32[16,256]{1,0:T(8,128)} custom-call(bf16[16,64,256]{2,1,0:T(8,128)(2,1)} %bitcast.8, s32[1,64]{1,0:T(1,128)} %inj.1, f32[16,256,256]{2,1,0:T(8,128)} %bitcast.6, f32[16,256,256]{2,1,0:T(8,128)} %bitcast.7, f32[1,256]{1,0:T(1,128)} %vel.1, f32[1,1]{1,0:T(1,128)} %bitcast.5.ew, bf16[256,1024]{1,0:T(8,128)(2,1)} %basis.1), custom_call_target="tpu_custom_call" | custom-call | tf_op jit(solution)/shard_map/pallas_call | solution.py:554
  30.1 1.3 %copy.10 = f32[256,16]{0,1:T(8,128)} copy(f32[256,16]{0,1:T(8,128)} %bitcast.9) | data formatting | bytes 32768

commit v3 on v2

--- a/solution.py
+++ b/solution.py
@@ -60,12 +60,16 @@
     all_slabs = n * slabs
     small = 2.0 / (all_slabs * cols * modes * groups * 4096.0)
 
-    def factor_in(s):
-        return pltpu.make_async_copy(fac_hbm.at[s], fac.at[s], fac_sem.at[s])
-
-    for i in range(half):
-        for k in range(2):
-            factor_in(k * half + half - 1 - i).start()
+    starts = {}
+    top = half
+    for size in (1, 1, 2, slabs):
+        size = min(size, top)
+        if size:
+            starts[top - 1] = pltpu.make_async_copy(
+                fac_hbm.at[:, top - size : top], fac.at[:, top - size : top], fac_sem.at[len(starts)]
+            )
+            starts[top - 1].start()
+            top = top - size
     pivots_in = pltpu.make_async_copy(piv_hbm, piv, piv_sem)
     pivots_in.start()
 
@@ -92,7 +96,8 @@
 
     cur[...] = jnp.zeros_like(cur)
 
-    def bring(s):
+    def bring(k, i):
+        s = k * half + i
         w = wave[s].astype(F32)
         sw = scaled_ref[...] * w
         sq = sw * w
@@ -106,15 +111,15 @@
         h, l = split(sw * small)
         srh[s] = h
         srl[s] = l
-        factor_in(s).wait()
-        h, l = split(fac[s])
+        h, l = split(fac[k, i])
         fh[s] = h
         fl[s] = l
         return h, l
 
+    starts[half - 1].wait()
     for k in range(2):
         end = k * half + half - 1
-        h, l = bring(end)
+        h, l = bring(k, half - 1)
         uh[end] = h
         ul[end] = l
         off[k] = jnp.zeros((cols, modes), F32)
@@ -125,7 +130,9 @@
         )
 
     def chain(i, carry):
-        blocks = [bring(k * half + half - 2 - i) for k in range(2)]
+        if half - 2 - i in starts:
+            starts[half - 2 - i].wait()
+        blocks = [bring(k, half - 2 - i) for k in range(2)]
         moved = []
         for k in range(2):
             s = k * half + half - 2 - i
@@ -557,7 +564,7 @@
         in_specs=[vmem, vmem, hbm, hbm, vmem, vmem, vmem],
         out_specs=vmem,
         scratch_shapes=[
-            full(slabs, modes, modes),
+            full(2, slabs // 2, modes, modes),
             full(slabs, modes, modes),
             short(slabs // 4, 8 * cols, modes),
             dma((slabs,)),
@@ -606,7 +613,7 @@
     )(
         wavefunction[0],
         injected_modes,
-        factor_blocks[0],
+        factor_blocks.reshape(2, slabs // 2, modes, modes),
         pivot_inverse[0],
         mode_velocity,
         energy_weight.reshape(1, 1),

time: 31.7 us -> 31.2 us (0.984)
  Pallas kernels: 29.4 us -> 28.9 us
    pallas_call x1, Pallas kernels: 29.4 us -> 28.9 us  [local(): pl.pallas_call(functools.partial(kernel, n, groups), out_shape=jax.ShapeD...]
where the time goes in v3:
time: 31.2 us; the launch traced here: 30.9 us
  Pallas kernels  28.9 us (93%)
  local copies, waits for them, and re-layouts  1.32 us (4%)
  between operations  0.66 us (2%)
    pallas_call x1, Pallas kernels, local(): pl.pallas_call(functools.partial(kernel, n, groups), out_shape=jax.ShapeD...  28.9 us
    unnamed x1, local copies, waits for them, and re-layouts  1.32 us

profile of v3, /device:TPU:0, one launch (start us, length us, event | category | flops | bytes accessed | tf_op | source)
XLA Modules:
  0.0 30.9 jit_solution(9221787777118577022)
XLA Ops:
  0.7 28.9 %shard_map.73 = f32[16,256]{1,0:T(8,128)} custom-call(bf16[16,64,256]{2,1,0:T(8,128)(2,1)} %bitcast.8, s32[1,64]{1,0:T(1,128)} %inj.1, f32[2,8,256,256]{3,2,1,0:T(8,128)} %bitcast.6, f32[16,256,256]{2,1,0:T(8,128)} %bitcast.7, f32[1,256]{1,0:T(1,128)} %vel.1, f32[1,1]{1,0:T(1,128)} %bitcast.5.ew, bf16[256,1024]{1,0:T(8,128)(2,1)} %basis.1), custom_call_target="tpu_custom_call" | custom-call | tf_op jit(solution)/shard_map/pallas_call | solution.py:561
  29.6 1.3 %copy.10 = f32[256,16]{0,1:T(8,128)} copy(f32[256,16]{0,1:T(8,128)} %bitcast.9) | data formatting | bytes 32768

commit v4 on v3

--- a/solution.py
+++ b/solution.py
@@ -38,7 +38,7 @@
     wave, inj, fac_hbm, piv_hbm, vel, ew, basis,
     out,
     fac, piv, ahl, fac_sem, piv_sem,
-    fh, fl, uh, ul, vh, vl, xh, xl, th, tl, zh, zl, wh, wl, gh, gl, srh, srl,
+    fh, fl, uh, ul, vh, vl, xh, xl, th, tl, zh, zl, wh, wl, gh, gl, kh, kl, qh, ql, bh, bl, srh, srl,
     rest, adj, wg, off, scaled_ref, whole_off, chip_off, local_e, exit_own,
     inc, incb, cinc, cur,
     po_s, po_r, pu_s, pu_r, pg_s, pg_r, osend, orecv, tsend, trecv, urecv, csend, crecv,
@@ -155,31 +155,34 @@
             vl[end] = l
             rest[end] = jnp.zeros((cols, modes), F32)
 
-    def climb(i, carry):
-        firsts = []
-        for k in range(2):
-            s = k * half + half - 2 - i
-            first = extended(s, fh[s], fl[s], vh[s + 1], vl[s + 1])
-            firsts.append(jnp.concatenate([first[0:modes], first[modes:] + rest[s + 1]], axis=0))
-        seconds = []
-        for k in range(2):
-            s = k * half + half - 2 - i
-            seconds.append(mm(firsts[k], fh[s], fl[s], True))
-        for k in range(2):
-            s = k * half + half - 2 - i
-            h, l = split(piv[s] + seconds[k][0:modes])
-            vh[s] = h
-            vl[s] = l
-            rest[s] = seconds[k][modes:]
-        return carry
-
-    beside = (half - 1) // 2 + -1
+    def lower(k, i):
+        s = k * half + half - 2 - i
+        first = extended(s, fh[s], fl[s], vh[s + 1], vl[s + 1])
+        return s, jnp.concatenate([first[0:modes], first[modes:] + rest[s + 1]], axis=0)
+
+    def place(s, second):
+        value = piv[s] + second[0:modes]
+        h, l = split(value)
+        vh[s] = h
+        vl[s] = l
+        rest[s] = second[modes:]
+        return value
+
+    def climb(i):
+        firsts = [lower(1, i)]
+        if i > 0:
+            firsts.append(lower(0, i - 1))
+        seconds = [mm(first, fh[s], fl[s], True) for s, first in firsts]
+        for (s, first), second in zip(firsts, seconds):
+            place(s, second)
+
+    beside = 2
     for i in range(half - 1):
         chain(i, 0)
         if i == half - 2 - beside:
             settle_ends()
         elif i > half - 2 - beside:
-            climb(i - (half - 1 - beside), 0)
+            climb(i - (half - 1 - beside))
 
     def copy_to(source, target, send, receive, device):
         return pltpu.make_async_remote_copy(
@@ -279,17 +282,18 @@
         wh[...] = h
         wl[...] = l
 
-    early = min(beside + 2, half - 1)
+    early = min(beside + 1, half - 1)
     for i in range(beside, early):
-        climb(i, 0)
+        climb(i)
 
     def carry_on():
         csend[...] = mm(cinc[...], wh[...], wl[...]) + chip_off[...]
+
+        @pl.when(chip < chips - 2)
+        def _():
+            carried_to(1).start()
+
         carried_to(0).start()
-
-        @pl.when(chip < chips - 2)
-        def _():
-            carried_to(1).start()
 
     cinc[...] = jnp.zeros_like(cinc)
 
@@ -310,18 +314,20 @@
                     transfer_to(j).start()
 
     for i in range(early, half - 1):
-        climb(i, 0)
+        climb(i)
 
     row_h, row_l = split(srh[half].astype(F32) + srl[half].astype(F32) + off_a)
-    first = mm_split(
+    joint = mm_split(
         jnp.concatenate([uh[0], row_h], axis=0),
         jnp.concatenate([ul[0], row_l], axis=0),
         vh[half], vl[half],
     )
-    first = jnp.concatenate([first[0:modes], first[modes:] + rest[half]], axis=0)
-    second = mm(first, uh[0], ul[0], True)
-    own_g = second[0:modes] + vh[0].astype(F32) + vl[0].astype(F32)
-    own_e = second[modes:] + rest[0] + mm_split(srh[0], srl[0], vh[0], vl[0])
+    joint = jnp.concatenate([joint[0:modes], joint[modes:] + rest[half]], axis=0)
+    _, first = lower(0, half - 2)
+    second = mm(first, fh[0], fl[0], True)
+    joint = mm(joint, uh[0], ul[0], True)
+    own_g = joint[0:modes] + place(0, second)
+    own_e = joint[modes:] + rest[0] + mm_split(srh[0], srl[0], vh[0], vl[0])
 
     @pl.when(core == 0)
     def _():
@@ -337,18 +343,27 @@
         gh[...] = h
         gl[...] = l
         local_e[...] = own_e
+        pair_g.wait_recv()
+        h, l = split(pg_r[0:modes])
+        kh[...] = h
+        kl[...] = l
 
         @pl.when(chip > 1)
         def _():
-            carried_to(0).wait_recv()
-            cinc[...] = crecv[...]
-
             @pl.when(odd == 1)
             def _():
                 offset_on.wait_recv()
                 transfer_on.wait_recv()
                 h, l = split(urecv[...])
-                cinc[...] = mm(cinc[...], h, l) + orecv[...]
+                qh[...] = h
+                ql[...] = l
+
+            carried_to(0).wait_recv()
+            cinc[...] = crecv[...]
+
+            @pl.when(odd == 1)
+            def _():
+                cinc[...] = mm(cinc[...], qh[...], ql[...]) + orecv[...]
 
                 @pl.when(chip < chips - 1)
                 def _():
@@ -358,13 +373,11 @@
         entry.start()
         inc[...] = mm(cinc[...], zh[...], zl[...]) + po_r[0:cols]
         exit_own[...] = local_e[...] + mm(inc[...], gh[...], gl[...])
-        pair_g.wait_recv()
 
         @pl.when(chip > 0)
         def _():
-            h, l = split(pg_r[0:modes])
             ysend[...] = (
-                pg_r[modes:] + mm(cinc[...], h, l) + mm(exit_own[...], zh[...], zl[...], True)
+                pg_r[modes:] + mm(cinc[...], kh[...], kl[...]) + mm(exit_own[...], zh[...], zl[...], True)
             )
             for j in range(chips):
                 @pl.when(j < chip)
@@ -384,7 +397,7 @@
             xl[s] = ul[s].T
         return tuple(following)
 
-    lax.fori_loop(0, half, settle, (inc[...], incb[...]), unroll=2)
+    lax.fori_loop(0, half, settle, (inc[...], incb[...]), unroll=4)
 
     def waves(b, carry):
         wg[b] = dot(wave[pl.ds(4 * b, 4)].reshape(4 * cols, modes), basis[...])
@@ -404,18 +417,23 @@
             def _():
                 share_to(d).start()
 
+        for j in range(chips - 2, 0, -1):
+            @pl.when(chip < j)
+            def _():
+                wait_transfer(j)
+                h, l = split(trecv[j].T)
+                bh[j] = h
+                bl[j] = l
+
         inc[...] = jnp.zeros_like(inc)
         for j in range(chips - 1, 0, -1):
             @pl.when(chip < j)
             def _():
-                if j < chips - 1:
-                    wait_transfer(j)
                 wait_exit(j)
                 if j == chips - 1:
                     inc[...] = yrecv[j]
                 else:
-                    h, l = split(trecv[j])
-                    inc[...] = mm(inc[...], h, l, True) + yrecv[j]
+                    inc[...] = mm(inc[...], bh[j], bl[j]) + yrecv[j]
 
         jsend[...] = exit_own[...] + mm(inc[...], th[...], tl[...], True)
         joining.start()
@@ -482,6 +500,56 @@
 
     current = jnp.sum(cur[...])
     factor = (all_slabs * grid * (2.0 / small)) / current
+    for copy in copies:
+        copy.wait_send()
+
+    @pl.when(core == 0)
+    def _():
+        pair_off.wait_send()
+        pair_u.wait_send()
+        pair_g.wait_send()
+
+    @pl.when(core == 1)
+    def _():
+        entry.wait_send()
+        joining.wait_send()
+        for k in range(1, groups):
+            tile_to(k).wait_send()
+        for d in range(n):
+            @pl.when(me != d)
+            def _():
+                share_to(d).wait_send()
+
+        @pl.when(onward)
+        def _():
+            offset_on.wait_send()
+
+        @pl.when(jnp.logical_and(onward, chip > 0))
+        def _():
+            transfer_on.wait_send()
+
+        @pl.when(jnp.logical_and(odd == 1, chip < chips - 1))
+        def _():
+            carried_to(0).wait_send()
+
+            @pl.when(chip < chips - 2)
+            def _():
+                carried_to(1).wait_send()
+
+        @pl.when(inner)
+        def _():
+            for j in range(chips):
+                @pl.when(j < chip)
+                def _():
+                    transfer_to(j).wait_send()
+
+        @pl.when(chip > 0)
+        def _():
+            for j in range(chips):
+                @pl.when(j < chip)
+                def _():
+                    exit_to(j).wait_send()
+
     summed = esend[groups - 1]
     for k in range(1, groups):
         pltpu.make_async_remote_copy(
@@ -490,55 +558,6 @@
         ).wait_recv()
         summed = summed + erecv[k]
     out[...] = summed * factor
-    for copy in copies:
-        copy.wait_send()
-
-    @pl.when(core == 0)
-    def _():
-        pair_off.wait_send()
-        pair_u.wait_send()
-        pair_g.wait_send()
-
-    @pl.when(core == 1)
-    def _():
-        entry.wait_send()
-        joining.wait_send()
-        for k in range(1, groups):
-            tile_to(k).wait_send()
-        for d in range(n):
-            @pl.when(me != d)
-            def _():
-                share_to(d).wait_send()
-
-        @pl.when(onward)
-        def _():
-            offset_on.wait_send()
-
-        @pl.when(jnp.logical_and(onward, chip > 0))
-        def _():
-            transfer_on.wait_send()
-
-        @pl.when(jnp.logical_and(odd == 1, chip < chips - 1))
-        def _():
-            carried_to(0).wait_send()
-
-            @pl.when(chip < chips - 2)
-            def _():
-                carried_to(1).wait_send()
-
-        @pl.when(inner)
-        def _():
-            for j in range(chips):
-                @pl.when(j < chip)
-                def _():
-                    transfer_to(j).wait_send()
-
-        @pl.when(chip > 0)
-        def _():
-            for j in range(chips):
-                @pl.when(j < chip)
-                def _():
-                    exit_to(j).wait_send()
 
 
 def local(wavefunction, injected_modes, factor_blocks, pivot_inverse, mode_velocity, energy_weight, mode_basis):
@@ -571,7 +590,8 @@
             dma,
         ]
         + [short(slabs, modes, modes)] * 8
-        + [short(modes, modes)] * 8
+        + [short(modes, modes)] * 12
+        + [short(chips, modes, modes)] * 2
         + [short(slabs, cols, modes)] * 2
         + [full(slabs, cols, modes)] * 2
         + [

time: 31.2 us -> 31 us (level)
  no operation moved by 1% of the time
where the time goes in v4:
time: 31 us; the launch traced here: 30.8 us
  Pallas kernels  28.8 us (93%)
  local copies, waits for them, and re-layouts  1.32 us (4%)
  between operations  0.66 us (2%)
    pallas_call x1, Pallas kernels, local(): pl.pallas_call(functools.partial(kernel, n, groups), out_shape=jax.ShapeD...  28.8 us
    unnamed x1, local copies, waits for them, and re-layouts  1.32 us

profile of v4, /device:TPU:0, one launch (start us, length us, event | category | flops | bytes accessed | tf_op | source)
XLA Modules:
  0.0 30.8 jit_solution(1105917229196735620)
XLA Ops:
  0.7 28.8 %shard_map.73 = f32[16,256]{1,0:T(8,128)} custom-call(bf16[16,64,256]{2,1,0:T(8,128)(2,1)} %bitcast.8, s32[1,64]{1,0:T(1,128)} %inj.1, f32[2,8,256,256]{3,2,1,0:T(8,128)} %bitcast.6, f32[16,256,256]{2,1,0:T(8,128)} %bitcast.7, f32[1,256]{1,0:T(1,128)} %vel.1, f32[1,1]{1,0:T(1,128)} %bitcast.5.ew, bf16[256,1024]{1,0:T(8,128)(2,1)} %basis.1), custom_call_target="tpu_custom_call" | custom-call | tf_op jit(solution)/shard_map/pallas_call | solution.py:580
  29.4 1.3 %copy.10 = f32[256,16]{0,1:T(8,128)} copy(f32[256,16]{0,1:T(8,128)} %bitcast.9) | data formatting | bytes 32768
